TPU v7x, 768 devices: a whole 4x8x12 slice. The times are simulated.
768 devices in a mesh: dp: 96 (over z, x, core), lists: 8 (over y).
Axes of the slice: x: 4, y: 8, z: 12, core: 2. Of those that a mesh axis runs over, the one named last changes fastest.
Arguments:
- pooled: bfloat16 [196608, 4096], P(('dp', 'lists')), may hold values from -6 to 6
- proj_weight: bfloat16 [4096, 1024], replicated, may hold values from -0.09375 to 0.09375
- centroids: bfloat16 [49152, 1024], P(('dp', 'lists')), may hold values from -6 to 6
- list_slot: int32 [196608], P(('dp', 'lists')), may hold values from 0 to 63
- pq_codes: int32 [196608, 64], P(('dp', 'lists')), may hold values from 0 to 255
- route_counts: int32 [768, 8], P(('dp', 'lists')), may hold values from 1 to 64, as said below
Outputs:
- new_centroids: float32 [49152, 1024], P(('dp', 'lists'))
- codebook: float32 [64, 16, 256], P('lists')
Inputs may be any that keep to these rules, and one draw needn't show every extreme that they name: `route_counts`: row b gives how many rows of device block b, in order, go to each lists index of its dp group; each row sums to 256 and holds one entry equal to 64, at the same position for all blocks of one dp index.
All inputs are finite; a program needn't handle non-finite values.
Results may differ from a plain program's by a relative error of at most 0.0038.
Values may be sent and summed in bfloat16 or wider, within the bound.
A program may use at most 64 MiB of HBM per device.

v0:
```python
import jax
import jax.numpy as jnp
from jax import lax
from jax.sharding import PartitionSpec as P

SUB = 64
CODES = 256
SUBW = 16


def pack_slots(values, counts_here, starts, capacity, fill):
    row_count = values.shape[0]
    slot_index = jnp.arange(capacity, dtype=jnp.int32)
    filled = slot_index[None, :] < counts_here[:, None]
    source = jnp.clip(starts[:, None] + slot_index[None, :], 0, row_count - 1)
    picked = values[source]
    if picked.ndim == 3:
        return jnp.where(filled[:, :, None], picked, jnp.full((), fill, picked.dtype))
    return jnp.where(filled, picked, jnp.full((), fill, picked.dtype))


def code_partials(residual, codes):
    row_count = residual.shape[0]
    code_select = (codes[:, :, None] == jnp.arange(CODES, dtype=jnp.int32)[None, None, :]).astype(
        jnp.bfloat16
    )
    sub_rows = residual.reshape(row_count, SUB, SUBW)
    code_sums = jnp.einsum(
        "rms,rmk->msk", sub_rows, code_select, preferred_element_type=jnp.float32
    )
    code_tally = jnp.sum(code_select, axis=0, dtype=jnp.float32)
    return (code_sums, code_tally)


def slot_sums(slot_select, rows):
    list_sums = jnp.einsum("nl,nf->lf", slot_select, rows, preferred_element_type=jnp.float32)
    list_tally = jnp.sum(slot_select, axis=0, dtype=jnp.float32)
    return (list_sums, list_tally)


def local(pooled, proj_weight, centroids, list_slot, pq_codes, route_counts):
    owners = lax.axis_size("lists")
    row_count = pooled.shape[0]
    list_dev = centroids.shape[0]
    features = proj_weight.shape[1]
    capacity = 2 * row_count // owners
    projected = jnp.dot(pooled, proj_weight, preferred_element_type=jnp.float32)
    factor = lax.rsqrt(jnp.mean(projected * projected, axis=1, keepdims=True) + 1e-06)
    normed = (projected * factor).astype(jnp.bfloat16)
    counts_here = route_counts[0]
    ends = jnp.cumsum(counts_here)
    starts = ends - counts_here
    positions = jnp.arange(row_count, dtype=jnp.int32)
    target = jnp.sum((positions[:, None] >= ends[None, :]).astype(jnp.int32), axis=1)
    group_list = target * list_dev + list_slot
    piece = lax.all_gather(centroids, "lists", axis=0, tiled=True)
    columns = jnp.arange(piece.shape[0], dtype=jnp.int32)
    select = (group_list[:, None] == columns[None, :]).astype(jnp.bfloat16)
    assigned = jnp.dot(select, piece, preferred_element_type=jnp.float32)
    residual = (normed.astype(jnp.float32) - assigned).astype(jnp.bfloat16)
    code_sums, code_tally = code_partials(residual, pq_codes)
    send_rows = pack_slots(normed, counts_here, starts, capacity, 0)
    send_slots = pack_slots(list_slot, counts_here, starts, capacity, -1)
    recv_rows, recv_slots = (
        lax.all_to_all(send_rows, "lists", split_axis=0, concat_axis=0, tiled=True),
        lax.all_to_all(send_slots, "lists", split_axis=0, concat_axis=0, tiled=True),
    )
    slot_select = (
        recv_slots.reshape(-1)[:, None] == jnp.arange(list_dev, dtype=jnp.int32)[None, :]
    ).astype(jnp.bfloat16)
    list_sums, list_tally = slot_sums(slot_select, recv_rows.reshape(-1, features))
    share = SUB // owners
    code_sums, code_tally = lax.psum((code_sums, code_tally), ("dp", "lists"))
    first = lax.axis_index("lists") * share
    code_sums = lax.dynamic_slice_in_dim(code_sums, first, share, 0)
    code_tally = lax.dynamic_slice_in_dim(code_tally, first, share, 0)
    codebook = code_sums / (1.0 + code_tally)[:, None, :]
    new_centroids = (centroids.astype(jnp.float32) + list_sums) / (1.0 + list_tally)[:, None]
    return (new_centroids, codebook)


def solution(mesh):
    in_specs = (
        P(("dp", "lists"), None),
        P(),
        P(("dp", "lists"), None),
        P(("dp", "lists")),
        P(("dp", "lists"), None),
        P(("dp", "lists"), None),
    )
    out_specs = (P(("dp", "lists"), None), P("lists", None, None))
    return jax.shard_map(local, mesh=mesh, in_specs=in_specs, out_specs=out_specs, check_vma=False)
```

profile of v0, /device:TPU:1, one launch (start us, length us, event | category | flops | bytes accessed | tf_op | source)
XLA Modules:
  0.0 582.2 jit_solution(11503526391277065930)
XLA Ops:
  7.2 1.0 reduce-window.7
  8.2 0.7 bitcast_subtract_fusion
  8.8 0.1 compare_select_fusion.1
  8.9 0.1 reshape.170
  9.0 3.6 gather_fusion
  12.6 0.1 gather.9
  12.7 1.3 compare_select_fusion
  14.0 7.7 %all-to-all-start = ((s32[8,1,64]{2,1,0:T(1,128)}), s32[8,1,64]{2,1,0:T(1,128)S(1)}, u32[]{:S(2)}, u32[]{:S(2)}) async-start(s32[8,1,64]{2,1,0:T(1,128)} %compare_select_fusion), calls=%async_computation | async-start | bytes 8192 | tf_op jit(solution)/shard_map/all_to_all | solution.py:66
  21.7 0.0 all-gather.2.cloned.1.call-start
  21.7 0.7 all-gather.2.cloned.1.call-update
  22.4 5.8 multiply_reduce_fusion
  28.2 0.1 multiply_convert_fusion
  28.4 2.8 gather_fusion.1
  31.2 0.1 iota_compare_fusion.7
  31.2 2.4 broadcast_select_fusion
  33.6 6.6 %all-to-all-start.1 = ((bf16[8,64,1024]{2,1,0:T(8,128)(2,1)}), bf16[8,64,1024]{2,1,0:T(8,128)(2,1)}, u32[]{:S(2)}, u32[]{:S(2)}) async-start(bf16[8,64,1024]{2,1,0:T(8,128)(2,1)} %broadcast_select_fusion), calls=%async_computation.1 | async-start | bytes 2097152 | tf_op jit(solution)/shard_map/all_to_all | solution.py:65
  40.2 0.0 all-reduce.3.cloned.1.call-start
  40.3 0.1 convert_reduce_fusion.2
  40.4 3.4 convert_reduce_fusion
  43.8 0.5 broadcast.122
  44.3 0.7 reduce.3
  45.0 0.1 eq.20
  45.1 34.0 %all-gather.2.cloned.1.call-done = bf16[512,1024]{1,0:T(8,128)(2,1)} async-done(((bf16[64,1024]{1,0:T(8,128)(2,1)}), bf16[512,1024]{1,0:T(8,128)(2,1)}) %all-gather.2.cloned.1.call-update) | async-done | bytes 1048592 | tf_op jit(solution)/shard_map/all_gather | solution.py:56
  79.1 1.7 fusion.3
  80.8 0.2 copy.10
  81.0 5.1 fusion.1
  86.1 0.0 all-reduce.3.cloned.1.call-update
  86.1 0.1 convert_reduce_fusion.1
  86.3 2.2 fusion.4
  88.5 484.6 %all-reduce.3.cloned.1.call-done = (f32[64,16,256]{2,1,0:T(8,128)}, f32[64,256]{1,0:T(8,128)}) async-done(((f32[64,16,256]{2,1,0:T(8,128)}, f32[64,256]{1,0:T(8,128)}), (f32[64,16,256]{2,1,0:T(8,128)}, f32[64,256]{1,0:T(8,128)})) %all-reduce.3.cloned.1.call-update) | async-done | bytes 1114128 | tf_op jit(solution)/shard_map/psum | solution.py:73
  573.1 0.7 dynamic-slice_add_fusion
  573.8 1.6 dynamic-slice_divide_fusion
  (16 shorter events, 0.1 us)
Async XLA Ops:
  7.2 15.2 %copy-start = (bf16[256,4096]{1,0:T(8,128)(2,1)S(1)}, bf16[256,4096]{1,0:T(8,128)(2,1)}, u32[]{:S(2)}) copy-start(bf16[256,4096]{1,0:T(8,128)(2,1)} %param.6) | copy-start | bytes 6291460
  14.0 19.6 %all-to-all-start = ((s32[8,1,64]{2,1,0:T(1,128)}), s32[8,1,64]{2,1,0:T(1,128)S(1)}, u32[]{:S(2)}, u32[]{:S(2)}) async-start(s32[8,1,64]{2,1,0:T(1,128)} %compare_select_fusion), calls=%async_computation | async-start | bytes 8192 | tf_op jit(solution)/shard_map/all_to_all | solution.py:66
  21.7 57.4 %all-gather.2.cloned.1.call-start = ((), (), s32[]{:S(2)}) async-start(), calls=%async_computation.2 | async-start | bytes 1179648 | tf_op jit(solution)/shard_map/all_gather | solution.py:56
  28.2 3.0 copy-start.4
  28.2 12.2 %copy-start.1 = (s32[256]{0:T(256)S(1)}, s32[256]{0:T(256)}, u32[]{:S(2)}) copy-start(s32[256]{0:T(256)} %param.9) | copy-start | bytes 3076
  28.2 12.2 %copy-start.3 = (s32[256,64]{0,1:T(8,128)S(1)}, s32[256,64]{0,1:T(8,128)}, u32[]{:S(2)}) copy-start(s32[256,64]{0,1:T(8,128)} %param.10) | copy-start | bytes 196612
  31.2 55.1 %copy-start.2 = (bf16[64,1024]{1,0:T(8,128)(2,1)S(1)}, bf16[64,1024]{1,0:T(8,128)(2,1)}, u32[]{:S(2)}) copy-start(bf16[64,1024]{1,0:T(8,128)(2,1)} %param.8) | copy-start | bytes 393220
  33.6 52.7 %all-to-all-start.1 = ((bf16[8,64,1024]{2,1,0:T(8,128)(2,1)}), bf16[8,64,1024]{2,1,0:T(8,128)(2,1)}, u32[]{:S(2)}, u32[]{:S(2)}) async-start(bf16[8,64,1024]{2,1,0:T(8,128)(2,1)} %broadcast_select_fusion), calls=%async_computation.1 | async-start | bytes 2097152 | tf_op jit(solution)/shard_map/all_to_all | solution.py:65
  40.2 532.9 %all-reduce.3.cloned.1.call-start = ((), (), s32[]{:S(2)}) async-start(), calls=%async_computation.3 | async-start | bytes 2228224 | tf_op jit(solution)/shard_map/psum | solution.py:73
Sparse Core Ops, SparseCore 0:
  24.9 54.1 all-gather.1
  86.3 486.8 all-reduce.2
where the time goes:
time: 583 us; the launch traced here: 582 us
  waiting for transfers between devices  519 us (89%)
  matrix products  14.8 us (3%)
  starting transfers between devices  14.4 us (2%)
  between operations  14.1 us (2%)
  other arithmetic  12.2 us (2%)
  local copies, waits for them, and re-layouts  7.4 us (1%)
    psum x1, waiting for transfers between devices, local(): code_sums, code_tally = lax.psum((code_sums, code_tally), ('dp', 'lists'))  485 us
    all_gather x1, waiting for transfers between devices, local(): piece = lax.all_gather(centroids, 'lists', axis=0, tiled=True)  34 us
  transfers between devices with their start and end apart: 4, of which 2 were waited for; matrix products, arithmetic and copies ran while one was open for 4% of the time, Pallas kernels for 0%

commit v1 on v0

v1 whole, which is shorter than its diff:
```python
import functools

import jax
import jax.numpy as jnp
from jax import lax
from jax.experimental import pallas as pl
from jax.experimental.pallas import tpu as pltpu
from jax.sharding import PartitionSpec as P

SUB = 64
CODES = 256
SUBW = 16
CAP = 64
LANES = 128
MESH = pl.DeviceIdType.MESH
BF = jnp.bfloat16
F32 = jnp.float32
I32 = jnp.int32
K_PARTS = 4


def iota(shape, dim):
    return lax.broadcasted_iota(I32, shape, dim)


def hot(mask):
    return jnp.where(mask, 1.0, 0.0).astype(BF)


def dot(a, b):
    return jnp.dot(a, b, preferred_element_type=F32)


def dot_nt(a, b):
    return lax.dot_general(a, b, (((1,), (1,)), ((), ())), preferred_element_type=F32)


def kernel(
    n_z, n_xc, n_y,
    counts_ref, slot_ref, codes_ref, cent_ref, pooled_hbm, weight_hbm,
    newc_ref, book_ref,
    pooled_v, weight_v, normed_v, xt_v, call_v, own_v, res_v,
    tl_v, t1_r, t2_b, t2_r, t3_r,
    cd_b, cd_r, ls_b, ls_r, s1_b, s1_r, s2_b, s2_r, s3_r, s4_r,
    in_sem, tl_s, t2_s, t3_s, cd_s, ls_s, s1_s, s2_s, s3_s, s4_s,
):
    rows, features = normed_v.shape[0], res_v.shape[1]
    dp, y = lax.axis_index("dp"), lax.axis_index("lists")
    z, xc = dp // n_xc, dp % n_xc

    def at_xc(o):
        return z * n_xc + lax.rem(xc + o, n_xc)

    def at_y(o):
        return lax.rem(y + o, n_y)

    def at_z(o):
        return lax.rem(z + o, n_z) * n_xc + xc

    def send(src, dst, sems, o, device):
        return pltpu.make_async_remote_copy(
            src_ref=src, dst_ref=dst, send_sem=sems.at[0, o], recv_sem=sems.at[1, o],
            device_id=device, device_id_type=MESH,
        )

    def tally1(o):
        return send(tl_v.at[lax.rem(xc + o, n_xc)], t1_r.at[o], tl_s, o, (at_xc(o), y))

    def tally2(o):
        return send(t2_b.at[at_y(o)], t2_r.at[o], t2_s, o, (dp, at_y(o)))

    def tally3(o):
        return send(t3_r.at[z], t3_r.at[z], t3_s, o, (at_z(o), y))

    def codes_out(o):
        return send(cd_b.at[at_y(o)], cd_r.at[o], cd_s, o, (dp, at_y(o)))

    def lists_out(o):
        block = pl.ds(pl.multiple_of(at_y(o) * CAP, CAP), CAP)
        return send(ls_b.at[block], ls_r.at[o], ls_s, o, (dp, at_y(o)))

    def sums1(o):
        return send(s1_b.at[o], s1_r.at[o], s1_s, o, (at_xc(o), y))

    def sums2(o):
        return send(s2_b.at[at_y(o)], s2_r.at[o], s2_s, o, (dp, at_y(o)))

    def sums3(o):
        return send(s3_r.at[z], s3_r.at[z], s3_s, o, (at_z(o), y))

    def sums4(o):
        return send(s4_r.at[xc], s4_r.at[xc], s4_s, o, (at_xc(o), y))

    depth = weight_v.shape[1]
    loads = []
    for k in range(K_PARTS):
        cols = pl.ds(k * depth, depth)
        pair = (
            pltpu.make_async_copy(pooled_hbm.at[:, cols], pooled_v.at[k], in_sem.at[0, k]),
            pltpu.make_async_copy(weight_hbm.at[cols], weight_v.at[k], in_sem.at[1, k]),
        )
        for copy in pair:
            copy.start()
        loads.append(pair)

    barrier = pltpu.get_barrier_semaphore()
    for o in range(1, n_xc):
        pl.semaphore_signal(barrier, inc=1, device_id=(at_xc(o), y), device_id_type=MESH)
    for o in range(1, n_y):
        pl.semaphore_signal(barrier, inc=1, device_id=(dp, at_y(o)), device_id_type=MESH)
    for o in range(1, n_z):
        pl.semaphore_signal(barrier, inc=1, device_id=(at_z(o), y), device_id_type=MESH)

    slot = slot_ref[...]
    pos = iota((1, rows), 1)
    target = jnp.zeros((1, rows), I32)
    lane = iota((rows, LANES), 1) - (y % 2) * CAP
    row = iota((rows, LANES), 0)
    start = 0
    places = []
    for d in range(n_y):
        count = counts_ref[0, d]
        places.append(hot((row == lane + start) & (lane >= 0) & (lane < count)))
        start = start + count
        target = target + jnp.where(pos >= start, 1, 0)
    codes = codes_ref[...]
    extra = jnp.where(iota((16, rows), 0) == 0, slot + 1, 0)
    packed = dot(
        jnp.concatenate([codes, extra], 0).astype(F32).astype(BF), jnp.concatenate(places, 1)
    ).astype(BF)
    for d in range(n_y):
        cd_b[d] = packed[:, d * LANES : (d + 1) * LANES]

    r128, l128 = iota((LANES, LANES), 0), iota((LANES, LANES), 1)
    rep = hot(iota((LANES, CODES), 0) % 16 == iota((LANES, CODES), 1) % 16)
    pick = iota((LANES, CODES), 0) % 16 == iota((LANES, CODES), 1) // 16
    fold = hot(iota((8, LANES), 1) // 16 == iota((8, LANES), 0))
    step = iota((LANES, rows), 0) % 16
    for g in range(SUB // 8):
        wide = jnp.concatenate(
            [jnp.broadcast_to(codes[g * 8 + j : g * 8 + j + 1], (16, rows)) for j in range(8)], 0
        )
        pairs = dot_nt(hot(wide // 16 == step), hot(wide % 16 == step))
        pairs = jnp.where(r128 // 16 == l128 // 16, pairs, 0.0).astype(BF)
        spread = jnp.where(pick, dot(pairs, rep), 0.0).astype(BF)
        tally = dot(fold, spread)
        for j in range(8):
            tl_v[j, g : g + 1] = tally[j : j + 1]

    pl.semaphore_wait(barrier, n_xc + n_y + n_z - 3)
    for o in range(1, n_y):
        codes_out(o).start()
    for o in range(1, n_xc):
        tally1(o).start()

    for k in range(K_PARTS):
        for copy in loads[k]:
            copy.wait()
        part = dot(pooled_v[k], weight_v[k])
        if k == 0:
            res_v[...] = part
        else:
            res_v[...] += part
    acc = res_v[...]
    factor = lax.rsqrt(jnp.mean(acc * acc, axis=1, keepdims=True) + 1e-6)
    normed = (acc * factor).astype(BF)
    normed_v[:, :features] = normed
    normed_v[:, features:] = jnp.ones((rows, LANES), BF)

    group_list = target * CAP + slot
    ls_b[...] = dot(hot(iota((n_y * CAP, rows), 0) == group_list), normed_v[...]).astype(BF)
    for o in range(1, n_y):
        lists_out(o).start()

    xt_v[:, :rows] = normed_v[:, :features].T
    call_v[:, :rows] = codes

    own = tl_v[xc]
    for o in range(1, n_xc):
        tally1(o).wait_recv()
        own = own + t1_r[o]
    for d in range(n_y):
        t2_b[d] = own[d : d + 1]
    for o in range(1, n_y):
        tally2(o).start()

    cd_r[0] = cd_b[y]
    for o in range(1, n_y):
        codes_out(o).wait_recv()
    for p in range(n_y // 2):
        both = cd_r[2 * p].astype(F32) + cd_r[2 * p + 1].astype(F32)
        cols = slice(rows + p * LANES, rows + (p + 1) * LANES)
        call_v[:, cols] = both[:SUB].astype(I32)
        chosen = hot(iota((CAP, LANES), 0) + 1 == both[SUB : SUB + 1].astype(I32))
        minus = lax.dot_general(
            cent_ref[...], chosen, (((0,), (0,)), ((), ())), preferred_element_type=F32
        )
        xt_v[:, cols] = (-minus).astype(BF)

    all_rows = call_v.shape[1]
    low = iota((16, all_rows), 0)

    def code_sums(o, out, kind):
        dest = lax.rem(xc + o, n_xc)
        for d in range(n_y):
            m = d * n_xc + dest
            gap = jnp.broadcast_to(call_v[pl.ds(m, 1)], (16, all_rows)) - low
            select = jnp.concatenate([hot(gap == 16 * h) for h in range(CODES // 16)], 0)
            piece = xt_v[pl.ds(pl.multiple_of(m * SUBW, SUBW), SUBW)]
            out[d * SUBW : (d + 1) * SUBW] = dot_nt(piece, select).astype(kind)

    def remote_chunk(o, carry):
        code_sums(o, s1_b.at[o], BF)
        sums1(o).start()
        return carry

    lax.fori_loop(1, n_xc, remote_chunk, 0)
    code_sums(0, own_v, F32)

    total = t2_b[y]
    for o in range(1, n_y):
        tally2(o).wait_recv()
        total = total + t2_r[o]
    t3_r[z] = total
    for o in range(1, n_z):
        tally3(o).start()

    for o in range(1, n_xc):
        sums1(o).wait_recv()
    for d in range(n_y):
        part = slice(d * SUBW, (d + 1) * SUBW)
        run = own_v[part]
        for o in range(1, n_xc):
            run = run + s1_r[o, part].astype(F32)
        s2_b[d] = run
    for o in range(1, n_y):
        sums2(o).start()
    run = s2_b[y]
    for o in range(1, n_y):
        sums2(o).wait_recv()
        run = run + s2_r[o]
    s3_r[z] = run.astype(BF)
    for o in range(1, n_z):
        sums3(o).start()

    for o in range(1, n_y):
        lists_out(o).wait_recv()
    lists = ls_b[pl.ds(pl.multiple_of(y * CAP, CAP), CAP)].astype(F32)
    for o in range(1, n_y):
        lists = lists + ls_r[o].astype(F32)
    scale = 1.0 / (1.0 + lists[:, features : features + 1])
    newc_ref[...] = (cent_ref[...].astype(F32) + lists[:, :features]) * scale

    for o in range(1, n_z):
        tally3(o).wait_recv()
    for o in range(1, n_z):
        sums3(o).wait_recv()
    total, run = t3_r[0], s3_r[0].astype(F32)
    for i in range(1, n_z):
        total = total + t3_r[i]
        run = run + s3_r[i].astype(F32)
    s4_r[xc] = run / (1.0 + total)
    for o in range(1, n_xc):
        sums4(o).start()
    for o in range(1, n_xc):
        sums4(o).wait_recv()
    book_ref[...] = s4_r[...]

    for o in range(1, n_xc):
        tally1(o).wait_send()
        sums1(o).wait_send()
        sums4(o).wait_send()
    for o in range(1, n_y):
        codes_out(o).wait_send()
        lists_out(o).wait_send()
        tally2(o).wait_send()
        sums2(o).wait_send()
    for o in range(1, n_z):
        tally3(o).wait_send()
        sums3(o).wait_send()


def local(n_z, n_xc, pooled, proj_weight, centroids, list_slot, pq_codes, route_counts):
    n_y = lax.axis_size("lists")
    rows, din = pooled.shape
    features = proj_weight.shape[1]
    all_rows = rows + n_y * CAP
    wide = features + LANES
    share = SUB // n_y
    depth = din // K_PARTS
    sem = pltpu.SemaphoreType.DMA
    vmem = pl.BlockSpec(memory_space=pltpu.VMEM)
    return pl.pallas_call(
        functools.partial(kernel, n_z, n_xc, n_y),
        out_shape=(
            jax.ShapeDtypeStruct(centroids.shape, F32),
            jax.ShapeDtypeStruct((share, SUBW, CODES), F32),
        ),
        in_specs=[
            pl.BlockSpec(memory_space=pltpu.SMEM), vmem, vmem, vmem,
            pl.BlockSpec(memory_space=pl.ANY), pl.BlockSpec(memory_space=pl.ANY),
        ],
        out_specs=(vmem, vmem),
        scratch_shapes=[
            pltpu.VMEM((K_PARTS, rows, depth), BF),
            pltpu.VMEM((K_PARTS, depth, features), BF),
            pltpu.VMEM((rows, wide), BF),
            pltpu.VMEM((features, all_rows), BF),
            pltpu.VMEM((SUB, all_rows), I32),
            pltpu.VMEM((n_y * SUBW, CODES), F32),
            pltpu.VMEM((rows, features), F32),
            pltpu.VMEM((n_xc, n_y, CODES), F32),
            pltpu.VMEM((n_xc, n_y, CODES), F32),
            pltpu.VMEM((n_y, 1, CODES), F32),
            pltpu.VMEM((n_y, 1, CODES), F32),
            pltpu.VMEM((n_z, 1, CODES), F32),
            pltpu.VMEM((n_y, SUB + 16, LANES), BF),
            pltpu.VMEM((n_y, SUB + 16, LANES), BF),
            pltpu.VMEM((n_y * CAP, wide), BF),
            pltpu.VMEM((n_y, CAP, wide), BF),
            pltpu.VMEM((n_xc, n_y * SUBW, CODES), BF),
            pltpu.VMEM((n_xc, n_y * SUBW, CODES), BF),
            pltpu.VMEM((n_y, SUBW, CODES), F32),
            pltpu.VMEM((n_y, SUBW, CODES), F32),
            pltpu.VMEM((n_z, SUBW, CODES), BF),
            pltpu.VMEM((n_xc, SUBW, CODES), F32),
            sem((2, K_PARTS)), sem((2, n_xc)), sem((2, n_y)), sem((2, n_z)), sem((2, n_y)),
            sem((2, n_y)), sem((2, n_xc)), sem((2, n_y)), sem((2, n_z)), sem((2, n_xc)),
        ],
        compiler_params=pltpu.CompilerParams(
            collective_id=0, has_side_effects=True, vmem_limit_bytes=48 << 20
        ),
        name="step",
    )(route_counts, list_slot.reshape(1, rows), pq_codes.T, centroids, pooled, proj_weight)


def solution(mesh):
    n_xc = SUB // mesh.shape["lists"]
    in_specs = (
        P(("dp", "lists"), None),
        P(),
        P(("dp", "lists"), None),
        P(("dp", "lists")),
        P(("dp", "lists"), None),
        P(("dp", "lists"), None),
    )
    out_specs = (P(("dp", "lists"), None), P("lists", None, None))
    step = functools.partial(local, mesh.shape["dp"] // n_xc, n_xc)
    return jax.shard_map(step, mesh=mesh, in_specs=in_specs, out_specs=out_specs, check_vma=False)
```

time: 583 us -> 77.7 us (0.13)
  waiting for transfers between devices: 519 us -> 0 us
  Pallas kernels: 0 us -> 70.7 us
  matrix products: 14.8 us -> 0 us
  starting transfers between devices: 14.4 us -> 0 us
  between operations: 14.1 us -> 0.65 us
  other arithmetic: 12.2 us -> 0 us
    psum x1 -> x0, waiting for transfers between devices: 485 us -> none  [local(): code_sums, code_tally = lax.psum((code_sums, code_tally), ('dp', 'lists'))]
    pallas_call x0 -> x1, Pallas kernels: none -> 70.7 us  [local(): pl.pallas_call(functools.partial(kernel, n_z, n_xc, n_y), out_shape=(jax....]
    all_gather x1 -> x0, waiting for transfers between devices: 34 us -> none  [local(): piece = lax.all_gather(centroids, 'lists', axis=0, tiled=True)]
    dot_general x4 -> x0, matrix products: 14.8 us -> none  [the longest x1 5.79 us: local(): projected = jnp.dot(pooled, proj_weight, preferred_element_type=jnp.float32)]
    all_to_all x2 -> x0, starting transfers between devices: 14.3 us -> none  [the longest x1 7.65 us: local(): lax.all_to_all(send_slots, 'lists', split_axis=0, concat_axis=0, tiled=True)]
    gather x3 -> x0, local copies, waits for them, and re-layouts: 6.5 us -> none  [pack_slots(): picked = values[source]]
    unnamed x10 -> x12, local copies, waits for them, and re-layouts: 0.03 us -> 6.02 us
  transfers between devices with their start and end apart: 4 -> 0, of which waited for: 2 -> 0; matrix products, arithmetic and copies ran while one was open for 4% -> 0% of each run, Pallas kernels for 0% -> 0%
where the time goes in v1:
time: 77.7 us; the launch traced here: 77.4 us
  Pallas kernels  70.7 us (91%)
  local copies, waits for them, and re-layouts  6.02 us (8%)
    pallas_call x1, Pallas kernels, local(): pl.pallas_call(functools.partial(kernel, n_z, n_xc, n_y), out_shape=(jax....  70.7 us
    unnamed x12, local copies, waits for them, and re-layouts  6.02 us

profile of v1, /device:TPU:1, one launch (start us, length us, event | category | flops | bytes accessed | tf_op | source)
XLA Modules:
  0.0 77.4 jit_solution(3250365132640471799)
XLA Ops:
  0.6 0.0 copy-start
  0.6 1.6 %copy-done = bf16[256,4096]{1,0:T(8,128)(2,1)S(1)} copy-done((bf16[256,4096]{1,0:T(8,128)(2,1)S(1)}, bf16[256,4096]{1,0:T(8,128)(2,1)}, u32[]{:S(2)}) %copy-start) | copy-done | bytes 2097176
  2.2 0.0 copy-start.1
  2.2 0.9 %copy-done.1 = bf16[64,1024]{1,0:T(8,128)(2,1)S(1)} copy-done((bf16[64,1024]{1,0:T(8,128)(2,1)S(1)}, bf16[64,1024]{1,0:T(8,128)(2,1)}, u32[]{:S(2)}) %copy-start.1) | copy-done | bytes 131096
  3.1 0.0 copy-start.2
  3.1 0.8 %copy-done.2 = s32[256,64]{0,1:T(8,128)S(1)} copy-done((s32[256,64]{0,1:T(8,128)S(1)}, s32[256,64]{0,1:T(8,128)}, u32[]{:S(2)}) %copy-start.2) | copy-done | bytes 65560
  4.0 0.0 copy-start.3
  4.0 0.7 copy-done.3
  4.6 0.0 copy-start.4
  4.7 0.7 copy-done.4
  5.3 70.7 %step.1 = (f32[64,1024]{1,0:T(8,128)S(1)}, f32[8,16,256]{2,1,0:T(8,128)S(1)}) custom-call(s32[1,8]{1,0:T(1,128)S(1)} %copy-done.4, s32[1,256]{1,0:T(1,128)S(1)} %bitcast.3, s32[64,256]{1,0:T(8,128)S(1)} %bitcast.2, bf16[64,1024]{1,0:T(8,128)(2,1)S(1)} %copy-done.1, bf16[256,4096]{1,0:T(8,128)(2,1)S(1)} %copy-done, bf16[4096,1024]{1,0:T(8,128)(2,1)} %weight_hbm.1), custom_call_target="tpu_custom_call" | custom-call | tf_op jit(solution)/shard_map/step/pallas_call | solution.py:293
  76.0 0.7 copy.10
  76.8 0.7 copy.11
Async XLA Ops:
  0.6 1.6 %copy-start = (bf16[256,4096]{1,0:T(8,128)(2,1)S(1)}, bf16[256,4096]{1,0:T(8,128)(2,1)}, u32[]{:S(2)}) copy-start(bf16[256,4096]{1,0:T(8,128)(2,1)} %pooled_hbm.1) | copy-start | bytes 6291460
  2.2 0.9 %copy-start.1 = (bf16[64,1024]{1,0:T(8,128)(2,1)S(1)}, bf16[64,1024]{1,0:T(8,128)(2,1)}, u32[]{:S(2)}) copy-start(bf16[64,1024]{1,0:T(8,128)(2,1)} %cent_ref.1) | copy-start | bytes 393220
  3.1 0.8 %copy-start.2 = (s32[256,64]{0,1:T(8,128)S(1)}, s32[256,64]{0,1:T(8,128)}, u32[]{:S(2)}) copy-start(s32[256,64]{0,1:T(8,128)} %param.10) | copy-start | bytes 196612
  4.0 0.7 copy-start.3
  4.6 0.7 copy-start.4

commit v2 on v1

--- a/solution.py
+++ b/solution.py
@@ -37,12 +37,13 @@
 
 def kernel(
     n_z, n_xc, n_y,
-    counts_ref, slot_ref, codes_ref, cent_ref, pooled_hbm, weight_hbm,
+    counts_hbm, slot_hbm, codes_hbm, cent_hbm, pooled_hbm, weight_hbm,
     newc_ref, book_ref,
+    counts_ref, slot_ref, codes_ref, cent_ref,
     pooled_v, weight_v, normed_v, xt_v, call_v, own_v, res_v,
     tl_v, t1_r, t2_b, t2_r, t3_r,
-    cd_b, cd_r, ls_b, ls_r, s1_b, s1_r, s2_b, s2_r, s3_r, s4_r,
-    in_sem, tl_s, t2_s, t3_s, cd_s, ls_s, s1_s, s2_s, s3_s, s4_s,
+    cd_b, cd_r, ls_b, up_r, down_r, tally_v, s1_b, s1_r, s2_b, s2_r, s3_r, s4_r,
+    in_sem, small_sem, tl_s, t2_s, t3_s, cd_s, up_s, down_s, s1_s, s2_s, s3_s, s4_s,
 ):
     rows, features = normed_v.shape[0], res_v.shape[1]
     dp, y = lax.axis_index("dp"), lax.axis_index("lists")
@@ -75,9 +76,31 @@
     def codes_out(o):
         return send(cd_b.at[at_y(o)], cd_r.at[o], cd_s, o, (dp, at_y(o)))
 
-    def lists_out(o):
-        block = pl.ds(pl.multiple_of(at_y(o) * CAP, CAP), CAP)
-        return send(ls_b.at[block], ls_r.at[o], ls_s, o, (dp, at_y(o)))
+    far = n_y // 2
+    half = features // 2
+
+    def block(o):
+        return pl.ds(pl.multiple_of(at_y(o) * CAP, CAP), CAP)
+
+    def ring(s, up):
+        dest = block(far + 1 - s if up else n_y - far - 1 + s)
+        slots, sems = (up_r, up_s) if up else (down_r, down_s)
+        src, dst = ls_b.at[dest], slots.at[s - 1]
+        if s == 1:
+            cols = pl.ds(0 if up else half, half)
+            src, dst = src.at[:, cols], dst.at[:, cols]
+        return send(src, dst, sems, s - 1, (dp, at_y(1 if up else n_y - 1)))
+
+    def ring_step(s):
+        for up in (True, False):
+            ring(s - 1, up).wait_recv()
+            dest = block(far + 1 - s if up else n_y - far - 1 + s)
+            cols = slice(0, features)
+            if s == 2:
+                cols = slice(0, half) if up else slice(half, features)
+            came = (up_r if up else down_r)[s - 2, :, cols].astype(F32)
+            ls_b[dest, cols] = (ls_b[dest, cols].astype(F32) + came).astype(BF)
+            ring(s, up).start()
 
     def sums1(o):
         return send(s1_b.at[o], s1_r.at[o], s1_s, o, (at_xc(o), y))
@@ -91,6 +114,19 @@
     def sums4(o):
         return send(s4_r.at[xc], s4_r.at[xc], s4_s, o, (at_xc(o), y))
 
+    small = [
+        pltpu.make_async_copy(src, dst, small_sem.at[i])
+        for i, (src, dst) in enumerate(
+            (
+                (counts_hbm, counts_ref),
+                (slot_hbm, slot_ref),
+                (codes_hbm, codes_ref),
+                (cent_hbm, cent_ref),
+            )
+        )
+    ]
+    for copy in small:
+        copy.start()
     depth = weight_v.shape[1]
     loads = []
     for k in range(K_PARTS):
@@ -111,6 +147,8 @@
     for o in range(1, n_z):
         pl.semaphore_signal(barrier, inc=1, device_id=(at_z(o), y), device_id_type=MESH)
 
+    for copy in small:
+        copy.wait()
     slot = slot_ref[...]
     pos = iota((1, rows), 1)
     target = jnp.zeros((1, rows), I32)
@@ -131,6 +169,10 @@
     for d in range(n_y):
         cd_b[d] = packed[:, d * LANES : (d + 1) * LANES]
 
+    pl.semaphore_wait(barrier, n_xc + n_y + n_z - 3)
+    for o in range(1, n_y):
+        codes_out(o).start()
+
     r128, l128 = iota((LANES, LANES), 0), iota((LANES, LANES), 1)
     rep = hot(iota((LANES, CODES), 0) % 16 == iota((LANES, CODES), 1) % 16)
     pick = iota((LANES, CODES), 0) % 16 == iota((LANES, CODES), 1) // 16
@@ -146,10 +188,6 @@
         tally = dot(fold, spread)
         for j in range(8):
             tl_v[j, g : g + 1] = tally[j : j + 1]
-
-    pl.semaphore_wait(barrier, n_xc + n_y + n_z - 3)
-    for o in range(1, n_y):
-        codes_out(o).start()
     for o in range(1, n_xc):
         tally1(o).start()
 
@@ -163,30 +201,20 @@
             res_v[...] += part
     acc = res_v[...]
     factor = lax.rsqrt(jnp.mean(acc * acc, axis=1, keepdims=True) + 1e-6)
-    normed = (acc * factor).astype(BF)
-    normed_v[:, :features] = normed
-    normed_v[:, features:] = jnp.ones((rows, LANES), BF)
+    normed_v[...] = (acc * factor).astype(BF)
 
     group_list = target * CAP + slot
     ls_b[...] = dot(hot(iota((n_y * CAP, rows), 0) == group_list), normed_v[...]).astype(BF)
-    for o in range(1, n_y):
-        lists_out(o).start()
-
-    xt_v[:, :rows] = normed_v[:, :features].T
+    ring(1, True).start()
+    ring(1, False).start()
+
+    xt_v[:, :rows] = normed_v[...].T
     call_v[:, :rows] = codes
 
-    own = tl_v[xc]
-    for o in range(1, n_xc):
-        tally1(o).wait_recv()
-        own = own + t1_r[o]
-    for d in range(n_y):
-        t2_b[d] = own[d : d + 1]
-    for o in range(1, n_y):
-        tally2(o).start()
-
     cd_r[0] = cd_b[y]
     for o in range(1, n_y):
         codes_out(o).wait_recv()
+    members = jnp.zeros((CAP, LANES), F32)
     for p in range(n_y // 2):
         both = cd_r[2 * p].astype(F32) + cd_r[2 * p + 1].astype(F32)
         cols = slice(rows + p * LANES, rows + (p + 1) * LANES)
@@ -196,6 +224,8 @@
             cent_ref[...], chosen, (((0,), (0,)), ((), ())), preferred_element_type=F32
         )
         xt_v[:, cols] = (-minus).astype(BF)
+        members = members + chosen.astype(F32)
+    tally_v[...] = jnp.broadcast_to(jnp.sum(members, axis=1, keepdims=True), (CAP, LANES))
 
     all_rows = call_v.shape[1]
     low = iota((16, all_rows), 0)
@@ -214,8 +244,19 @@
         sums1(o).start()
         return carry
 
-    lax.fori_loop(1, n_xc, remote_chunk, 0)
-    code_sums(0, own_v, F32)
+    first, second = n_xc // 4 + 1, n_xc - 2
+    lax.fori_loop(1, first, remote_chunk, 0)
+
+    own = tl_v[xc]
+    for o in range(1, n_xc):
+        tally1(o).wait_recv()
+        own = own + t1_r[o]
+    for d in range(n_y):
+        t2_b[d] = own[d : d + 1]
+    for o in range(1, n_y):
+        tally2(o).start()
+    ring_step(2)
+    lax.fori_loop(first, second, remote_chunk, 0)
 
     total = t2_b[y]
     for o in range(1, n_y):
@@ -224,6 +265,9 @@
     t3_r[z] = total
     for o in range(1, n_z):
         tally3(o).start()
+    ring_step(3)
+    lax.fori_loop(second, n_xc, remote_chunk, 0)
+    code_sums(0, own_v, F32)
 
     for o in range(1, n_xc):
         sums1(o).wait_recv()
@@ -235,6 +279,8 @@
         s2_b[d] = run
     for o in range(1, n_y):
         sums2(o).start()
+    for s in range(4, far + 1):
+        ring_step(s)
     run = s2_b[y]
     for o in range(1, n_y):
         sums2(o).wait_recv()
@@ -243,13 +289,11 @@
     for o in range(1, n_z):
         sums3(o).start()
 
-    for o in range(1, n_y):
-        lists_out(o).wait_recv()
-    lists = ls_b[pl.ds(pl.multiple_of(y * CAP, CAP), CAP)].astype(F32)
-    for o in range(1, n_y):
-        lists = lists + ls_r[o].astype(F32)
-    scale = 1.0 / (1.0 + lists[:, features : features + 1])
-    newc_ref[...] = (cent_ref[...].astype(F32) + lists[:, :features]) * scale
+    lists = cent_ref[...].astype(F32) + ls_b[block(0)].astype(F32)
+    for up, slots in ((True, up_r), (False, down_r)):
+        ring(far, up).wait_recv()
+        lists = lists + slots[far - 1].astype(F32)
+    newc_ref[...] = lists * (1.0 / (1.0 + tally_v[:, :1]))
 
     for o in range(1, n_z):
         tally3(o).wait_recv()
@@ -272,9 +316,11 @@
         sums4(o).wait_send()
     for o in range(1, n_y):
         codes_out(o).wait_send()
-        lists_out(o).wait_send()
         tally2(o).wait_send()
         sums2(o).wait_send()
+    for s in range(1, far + 1):
+        ring(s, True).wait_send()
+        ring(s, False).wait_send()
     for o in range(1, n_z):
         tally3(o).wait_send()
         sums3(o).wait_send()
@@ -285,26 +331,28 @@
     rows, din = pooled.shape
     features = proj_weight.shape[1]
     all_rows = rows + n_y * CAP
-    wide = features + LANES
+    far = n_y // 2
     share = SUB // n_y
     depth = din // K_PARTS
     sem = pltpu.SemaphoreType.DMA
     vmem = pl.BlockSpec(memory_space=pltpu.VMEM)
+    hbm = pl.BlockSpec(memory_space=pltpu.HBM)
     return pl.pallas_call(
         functools.partial(kernel, n_z, n_xc, n_y),
         out_shape=(
             jax.ShapeDtypeStruct(centroids.shape, F32),
             jax.ShapeDtypeStruct((share, SUBW, CODES), F32),
         ),
-        in_specs=[
-            pl.BlockSpec(memory_space=pltpu.SMEM), vmem, vmem, vmem,
-            pl.BlockSpec(memory_space=pl.ANY), pl.BlockSpec(memory_space=pl.ANY),
-        ],
+        in_specs=[hbm] * 6,
         out_specs=(vmem, vmem),
         scratch_shapes=[
+            pltpu.SMEM((1, n_y), I32),
+            pltpu.VMEM((1, rows), I32),
+            pltpu.VMEM((SUB, rows), I32),
+            pltpu.VMEM(centroids.shape, BF),
             pltpu.VMEM((K_PARTS, rows, depth), BF),
             pltpu.VMEM((K_PARTS, depth, features), BF),
-            pltpu.VMEM((rows, wide), BF),
+            pltpu.VMEM((rows, features), BF),
             pltpu.VMEM((features, all_rows), BF),
             pltpu.VMEM((SUB, all_rows), I32),
             pltpu.VMEM((n_y * SUBW, CODES), F32),
@@ -316,19 +364,21 @@
             pltpu.VMEM((n_z, 1, CODES), F32),
             pltpu.VMEM((n_y, SUB + 16, LANES), BF),
             pltpu.VMEM((n_y, SUB + 16, LANES), BF),
-            pltpu.VMEM((n_y * CAP, wide), BF),
-            pltpu.VMEM((n_y, CAP, wide), BF),
+            pltpu.VMEM((n_y * CAP, features), BF),
+            pltpu.VMEM((far, CAP, features), BF),
+            pltpu.VMEM((far, CAP, features), BF),
+            pltpu.VMEM((CAP, LANES), F32),
             pltpu.VMEM((n_xc, n_y * SUBW, CODES), BF),
             pltpu.VMEM((n_xc, n_y * SUBW, CODES), BF),
             pltpu.VMEM((n_y, SUBW, CODES), F32),
             pltpu.VMEM((n_y, SUBW, CODES), F32),
             pltpu.VMEM((n_z, SUBW, CODES), BF),
             pltpu.VMEM((n_xc, SUBW, CODES), F32),
-            sem((2, K_PARTS)), sem((2, n_xc)), sem((2, n_y)), sem((2, n_z)), sem((2, n_y)),
-            sem((2, n_y)), sem((2, n_xc)), sem((2, n_y)), sem((2, n_z)), sem((2, n_xc)),
+            sem((2, K_PARTS)), sem((4,)), sem((2, n_xc)), sem((2, n_y)), sem((2, n_z)),
+            sem((2, n_y)), sem((2, far)), sem((2, far)), sem((2, n_xc)), sem((2, n_y)), sem((2, n_z)), sem((2, n_xc)),
         ],
         compiler_params=pltpu.CompilerParams(
-            collective_id=0, has_side_effects=True, vmem_limit_bytes=48 << 20
+            collective_id=0, has_side_effects=True, vmem_limit_bytes=63 << 20
         ),
         name="step",
     )(route_counts, list_slot.reshape(1, rows), pq_codes.T, centroids, pooled, proj_weight)

time: 77.7 us -> 64.2 us (0.83)
  Pallas kernels: 70.7 us -> 60.2 us
  local copies, waits for them, and re-layouts: 6.02 us -> 3.24 us
    pallas_call x1, Pallas kernels: 70.7 us -> 60.2 us  [local(): pl.pallas_call(functools.partial(kernel, n_z, n_xc, n_y), out_shape=(jax....]
    unnamed x12 -> x2, local copies, waits for them, and re-layouts: 6.02 us -> 3.24 us
where the time goes in v2:
time: 64.2 us; the launch traced here: 64 us
  Pallas kernels  60.2 us (94%)
  local copies, waits for them, and re-layouts  3.24 us (5%)
    pallas_call x1, Pallas kernels, local(): pl.pallas_call(functools.partial(kernel, n_z, n_xc, n_y), out_shape=(jax....  60.2 us
    unnamed x2, local copies, waits for them, and re-layouts  3.24 us

profile of v2, /device:TPU:1, one launch (start us, length us, event | category | flops | bytes accessed | tf_op | source)
XLA Modules:
  0.0 64.0 jit_solution(1831685863493219322)
XLA Ops:
  0.6 60.2 %step.1 = (f32[64,1024]{1,0:T(8,128)}, f32[8,16,256]{2,1,0:T(8,128)}) custom-call(s32[1,8]{1,0:T(1,128)} %counts_hbm.1, s32[1,256]{1,0:T(1,128)} %bitcast.3, s32[64,256]{1,0:T(8,128)} %bitcast.2, bf16[64,1024]{1,0:T(8,128)(2,1)} %cent_hbm.1, bf16[256,4096]{1,0:T(8,128)(2,1)} %pooled_hbm.1, bf16[4096,1024]{1,0:T(8,128)(2,1)} %weight_hbm.1), custom_call_target="tpu_custom_call" | custom-call | tf_op jit(solution)/shard_map/step/pallas_call | solution.py:340
  60.8 1.7 %copy.10 = f32[64,1024]{1,0:T(8,128)} copy(f32[64,1024]{1,0:T(8,128)} %get-tuple-element.4) | data formatting | bytes 524288
  62.5 1.6 %copy.11 = f32[8,16,256]{2,1,0:T(8,128)} copy(f32[8,16,256]{2,1,0:T(8,128)} %get-tuple-element.5) | data formatting | bytes 262144

commit v3 on v2

--- a/solution.py
+++ b/solution.py
@@ -17,6 +17,7 @@
 F32 = jnp.float32
 I32 = jnp.int32
 K_PARTS = 4
+QUAD = 4
 
 
 def iota(shape, dim):
@@ -41,9 +42,9 @@
     newc_ref, book_ref,
     counts_ref, slot_ref, codes_ref, cent_ref,
     pooled_v, weight_v, normed_v, xt_v, call_v, own_v, res_v,
-    tl_v, t1_r, t2_b, t2_r, t3_r,
-    cd_b, cd_r, ls_b, up_r, down_r, tally_v, s1_b, s1_r, s2_b, s2_r, s3_r, s4_r,
-    in_sem, small_sem, tl_s, t2_s, t3_s, cd_s, up_s, down_s, s1_s, s2_s, s3_s, s4_s,
+    tl_v, t1_r, t2_b, t2_r,
+    cd_b, cd_r, ls_b, up_r, down_r, tally_v, s1_b, s1_r, s2_b, s2_r, s3_r, s3b_r, s4_r,
+    in_sem, small_sem, tl_s, t2_s, cd_s, up_s, down_s, s1_s, s2_s, s3_s, s3b_s, s4_s,
 ):
     rows, features = normed_v.shape[0], res_v.shape[1]
     dp, y = lax.axis_index("dp"), lax.axis_index("lists")
@@ -55,8 +56,14 @@
     def at_y(o):
         return lax.rem(y + o, n_y)
 
-    def at_z(o):
-        return lax.rem(z + o, n_z) * n_xc + xc
+    n_q = n_z // QUAD
+    q, r = z // QUAD, z % QUAD
+
+    def at_q(o):
+        return (lax.rem(q + o, n_q) * QUAD + r) * n_xc + xc
+
+    def at_r(o):
+        return (q * QUAD + lax.rem(r + o, QUAD)) * n_xc + xc
 
     def send(src, dst, sems, o, device):
         return pltpu.make_async_remote_copy(
@@ -69,9 +76,6 @@
 
     def tally2(o):
         return send(t2_b.at[at_y(o)], t2_r.at[o], t2_s, o, (dp, at_y(o)))
-
-    def tally3(o):
-        return send(t3_r.at[z], t3_r.at[z], t3_s, o, (at_z(o), y))
 
     def codes_out(o):
         return send(cd_b.at[at_y(o)], cd_r.at[o], cd_s, o, (dp, at_y(o)))
@@ -109,7 +113,10 @@
         return send(s2_b.at[at_y(o)], s2_r.at[o], s2_s, o, (dp, at_y(o)))
 
     def sums3(o):
-        return send(s3_r.at[z], s3_r.at[z], s3_s, o, (at_z(o), y))
+        return send(s3_r.at[q], s3_r.at[q], s3_s, o, (at_q(o), y))
+
+    def sums3b(o):
+        return send(s3b_r.at[r], s3b_r.at[r], s3b_s, o, (at_r(o), y))
 
     def sums4(o):
         return send(s4_r.at[xc], s4_r.at[xc], s4_s, o, (at_xc(o), y))
@@ -144,8 +151,10 @@
         pl.semaphore_signal(barrier, inc=1, device_id=(at_xc(o), y), device_id_type=MESH)
     for o in range(1, n_y):
         pl.semaphore_signal(barrier, inc=1, device_id=(dp, at_y(o)), device_id_type=MESH)
-    for o in range(1, n_z):
-        pl.semaphore_signal(barrier, inc=1, device_id=(at_z(o), y), device_id_type=MESH)
+    for o in range(1, n_q):
+        pl.semaphore_signal(barrier, inc=1, device_id=(at_q(o), y), device_id_type=MESH)
+    for o in range(1, QUAD):
+        pl.semaphore_signal(barrier, inc=1, device_id=(at_r(o), y), device_id_type=MESH)
 
     for copy in small:
         copy.wait()
@@ -169,7 +178,7 @@
     for d in range(n_y):
         cd_b[d] = packed[:, d * LANES : (d + 1) * LANES]
 
-    pl.semaphore_wait(barrier, n_xc + n_y + n_z - 3)
+    pl.semaphore_wait(barrier, n_xc + n_y + n_q + QUAD - 4)
     for o in range(1, n_y):
         codes_out(o).start()
 
@@ -258,13 +267,6 @@
     ring_step(2)
     lax.fori_loop(first, second, remote_chunk, 0)
 
-    total = t2_b[y]
-    for o in range(1, n_y):
-        tally2(o).wait_recv()
-        total = total + t2_r[o]
-    t3_r[z] = total
-    for o in range(1, n_z):
-        tally3(o).start()
     ring_step(3)
     lax.fori_loop(second, n_xc, remote_chunk, 0)
     code_sums(0, own_v, F32)
@@ -279,15 +281,36 @@
         s2_b[d] = run
     for o in range(1, n_y):
         sums2(o).start()
+    total = t2_b[y]
+    for o in range(1, n_y):
+        tally2(o).wait_recv()
+        total = total + t2_r[o]
+    run = s2_b[y]
+    for o in range(1, n_y):
+        sums2(o).wait_recv()
+        run = run + s2_r[o]
+    s3_r[q, :SUBW] = run
+    s3_r[q, SUBW:] = jnp.broadcast_to(total, (8, CODES))
+    for o in range(1, n_q):
+        sums3(o).start()
     for s in range(4, far + 1):
         ring_step(s)
-    run = s2_b[y]
-    for o in range(1, n_y):
-        sums2(o).wait_recv()
-        run = run + s2_r[o]
-    s3_r[z] = run.astype(BF)
-    for o in range(1, n_z):
-        sums3(o).start()
+    for o in range(1, n_q):
+        sums3(o).wait_recv()
+    run = s3_r[0]
+    for i in range(1, n_q):
+        run = run + s3_r[i]
+    s3b_r[r] = run
+    for o in range(1, QUAD):
+        sums3b(o).start()
+    for o in range(1, QUAD):
+        sums3b(o).wait_recv()
+    run = s3b_r[0]
+    for i in range(1, QUAD):
+        run = run + s3b_r[i]
+    s4_r[xc] = run[:SUBW] / (1.0 + run[SUBW : SUBW + 1])
+    for o in range(1, n_xc):
+        sums4(o).start()
 
     lists = cent_ref[...].astype(F32) + ls_b[block(0)].astype(F32)
     for up, slots in ((True, up_r), (False, down_r)):
@@ -295,17 +318,6 @@
         lists = lists + slots[far - 1].astype(F32)
     newc_ref[...] = lists * (1.0 / (1.0 + tally_v[:, :1]))
 
-    for o in range(1, n_z):
-        tally3(o).wait_recv()
-    for o in range(1, n_z):
-        sums3(o).wait_recv()
-    total, run = t3_r[0], s3_r[0].astype(F32)
-    for i in range(1, n_z):
-        total = total + t3_r[i]
-        run = run + s3_r[i].astype(F32)
-    s4_r[xc] = run / (1.0 + total)
-    for o in range(1, n_xc):
-        sums4(o).start()
     for o in range(1, n_xc):
         sums4(o).wait_recv()
     book_ref[...] = s4_r[...]
@@ -321,9 +333,10 @@
     for s in range(1, far + 1):
         ring(s, True).wait_send()
         ring(s, False).wait_send()
-    for o in range(1, n_z):
-        tally3(o).wait_send()
+    for o in range(1, n_q):
         sums3(o).wait_send()
+    for o in range(1, QUAD):
+        sums3b(o).wait_send()
 
 
 def local(n_z, n_xc, pooled, proj_weight, centroids, list_slot, pq_codes, route_counts):
@@ -335,6 +348,8 @@
     share = SUB // n_y
     depth = din // K_PARTS
     sem = pltpu.SemaphoreType.DMA
+    slots = list_slot.reshape(1, rows)
+    operands = (route_counts, slots, pq_codes.T, centroids, pooled, proj_weight)
     vmem = pl.BlockSpec(memory_space=pltpu.VMEM)
     hbm = pl.BlockSpec(memory_space=pltpu.HBM)
     return pl.pallas_call(
@@ -361,7 +376,6 @@
             pltpu.VMEM((n_xc, n_y, CODES), F32),
             pltpu.VMEM((n_y, 1, CODES), F32),
             pltpu.VMEM((n_y, 1, CODES), F32),
-            pltpu.VMEM((n_z, 1, CODES), F32),
             pltpu.VMEM((n_y, SUB + 16, LANES), BF),
             pltpu.VMEM((n_y, SUB + 16, LANES), BF),
             pltpu.VMEM((n_y * CAP, features), BF),
@@ -372,16 +386,18 @@
             pltpu.VMEM((n_xc, n_y * SUBW, CODES), BF),
             pltpu.VMEM((n_y, SUBW, CODES), F32),
             pltpu.VMEM((n_y, SUBW, CODES), F32),
-            pltpu.VMEM((n_z, SUBW, CODES), BF),
+            pltpu.VMEM((n_z // QUAD, SUBW + 8, CODES), F32),
+            pltpu.VMEM((QUAD, SUBW + 8, CODES), F32),
             pltpu.VMEM((n_xc, SUBW, CODES), F32),
-            sem((2, K_PARTS)), sem((4,)), sem((2, n_xc)), sem((2, n_y)), sem((2, n_z)),
-            sem((2, n_y)), sem((2, far)), sem((2, far)), sem((2, n_xc)), sem((2, n_y)), sem((2, n_z)), sem((2, n_xc)),
+            sem((2, K_PARTS)), sem((4,)), sem((2, n_xc)), sem((2, n_y)), sem((2, n_y)),
+            sem((2, far)), sem((2, far)), sem((2, n_xc)), sem((2, n_y)),
+            sem((2, n_z // QUAD)), sem((2, QUAD)), sem((2, n_xc)),
         ],
         compiler_params=pltpu.CompilerParams(
-            collective_id=0, has_side_effects=True, vmem_limit_bytes=63 << 20
+            collective_id=0, has_side_effects=True, vmem_limit_bytes=48 << 20
         ),
         name="step",
-    )(route_counts, list_slot.reshape(1, rows), pq_codes.T, centroids, pooled, proj_weight)
+    )(*(pltpu.with_memory_space_constraint(v, pltpu.HBM) for v in operands))
 
 
 def solution(mesh):

time: 64.2 us -> 62.3 us (0.970)
  local copies, waits for them, and re-layouts: 3.24 us -> 1.36 us
    unnamed x2, local copies, waits for them, and re-layouts: 3.24 us -> 1.36 us
where the time goes in v3:
time: 62.3 us; the launch traced here: 62.2 us
  Pallas kernels  60.2 us (97%)
  local copies, waits for them, and re-layouts  1.36 us (2%)
  between operations  0.64 us (1%)
    pallas_call x1, Pallas kernels, local(): pl.pallas_call(functools.partial(kernel, n_z, n_xc, n_y), out_shape=(jax....  60.2 us
    unnamed x2, local copies, waits for them, and re-layouts  1.36 us

profile of v3, /device:TPU:1, one launch (start us, length us, event | category | flops | bytes accessed | tf_op | source)
XLA Modules:
  0.0 62.2 jit_solution(12349016944421720386)
XLA Ops:
  0.6 60.2 %step.1 = (f32[64,1024]{1,0:T(8,128)S(1)}, f32[8,16,256]{2,1,0:T(8,128)S(1)}) custom-call(s32[1,8]{1,0:T(1,128)} %counts_hbm.1, s32[1,256]{1,0:T(1,128)} %bitcast.3, s32[64,256]{1,0:T(8,128)} %bitcast.2, bf16[64,1024]{1,0:T(8,128)(2,1)} %cent_hbm.1, bf16[256,4096]{1,0:T(8,128)(2,1)} %pooled_hbm.1, bf16[4096,1024]{1,0:T(8,128)(2,1)} %weight_hbm.1), custom_call_target="tpu_custom_call" | custom-call | tf_op jit(solution)/shard_map/step/pallas_call | solution.py:355
  60.8 0.7 %copy.10 = f32[64,1024]{1,0:T(8,128)} copy(f32[64,1024]{1,0:T(8,128)S(1)} %get-tuple-element.4) | data formatting | bytes 524288
  61.5 0.7 %copy.11 = f32[8,16,256]{2,1,0:T(8,128)} copy(f32[8,16,256]{2,1,0:T(8,128)S(1)} %get-tuple-element.5) | data formatting | bytes 262144

commit v4 on v2

--- a/solution.py
+++ b/solution.py
@@ -42,7 +42,7 @@
     counts_ref, slot_ref, codes_ref, cent_ref,
     pooled_v, weight_v, normed_v, xt_v, call_v, own_v, res_v,
     tl_v, t1_r, t2_b, t2_r, t3_r,
-    cd_b, cd_r, ls_b, up_r, down_r, tally_v, s1_b, s1_r, s2_b, s2_r, s3_r, s4_r,
+    cd_b, cd_r, centt_v, ls_b, up_r, down_r, tally_v, s1_b, s1_r, s2_b, s2_r, s3_r, s4_r,
     in_sem, small_sem, tl_s, t2_s, t3_s, cd_s, up_s, down_s, s1_s, s2_s, s3_s, s4_s,
 ):
     rows, features = normed_v.shape[0], res_v.shape[1]
@@ -69,9 +69,6 @@
 
     def tally2(o):
         return send(t2_b.at[at_y(o)], t2_r.at[o], t2_s, o, (dp, at_y(o)))
-
-    def tally3(o):
-        return send(t3_r.at[z], t3_r.at[z], t3_s, o, (at_z(o), y))
 
     def codes_out(o):
         return send(cd_b.at[at_y(o)], cd_r.at[o], cd_s, o, (dp, at_y(o)))
@@ -107,6 +104,9 @@
 
     def sums2(o):
         return send(s2_b.at[at_y(o)], s2_r.at[o], s2_s, o, (dp, at_y(o)))
+
+    def tally3(o):
+        return send(t3_r.at[z], t3_r.at[z], t3_s, o, (at_z(o), y))
 
     def sums3(o):
         return send(s3_r.at[z], s3_r.at[z], s3_s, o, (at_z(o), y))
@@ -152,8 +152,9 @@
     slot = slot_ref[...]
     pos = iota((1, rows), 1)
     target = jnp.zeros((1, rows), I32)
-    lane = iota((rows, LANES), 1) - (y % 2) * CAP
-    row = iota((rows, LANES), 0)
+    row = iota((2 * rows, LANES), 0)
+    lane = iota((2 * rows, LANES), 1) - row // rows * CAP
+    row = row % rows
     start = 0
     places = []
     for d in range(n_y):
@@ -162,16 +163,24 @@
         start = start + count
         target = target + jnp.where(pos >= start, 1, 0)
     codes = codes_ref[...]
+    codes_half = SUB // 2
     extra = jnp.where(iota((16, rows), 0) == 0, slot + 1, 0)
-    packed = dot(
-        jnp.concatenate([codes, extra], 0).astype(F32).astype(BF), jnp.concatenate(places, 1)
-    ).astype(BF)
+    halves = jnp.concatenate(
+        [
+            jnp.concatenate([codes[:codes_half], extra], 0),
+            jnp.concatenate([codes[codes_half:], jnp.zeros((16, rows), I32)], 0),
+        ],
+        1,
+    )
+    packed = dot(halves.astype(F32).astype(BF), jnp.concatenate(places, 1)).astype(BF)
     for d in range(n_y):
         cd_b[d] = packed[:, d * LANES : (d + 1) * LANES]
 
     pl.semaphore_wait(barrier, n_xc + n_y + n_z - 3)
     for o in range(1, n_y):
         codes_out(o).start()
+
+    centt_v[...] = (-cent_ref[...].astype(F32)).T.astype(BF)
 
     r128, l128 = iota((LANES, LANES), 0), iota((LANES, LANES), 1)
     rep = hot(iota((LANES, CODES), 0) % 16 == iota((LANES, CODES), 1) % 16)
@@ -214,17 +223,20 @@
     cd_r[0] = cd_b[y]
     for o in range(1, n_y):
         codes_out(o).wait_recv()
+    low_lanes = iota((codes_half + 16, LANES), 1) < CAP
+    picks = []
     members = jnp.zeros((CAP, LANES), F32)
     for p in range(n_y // 2):
-        both = cd_r[2 * p].astype(F32) + cd_r[2 * p + 1].astype(F32)
+        left, right = cd_r[2 * p].astype(F32), cd_r[2 * p + 1].astype(F32)
+        upper = jnp.where(low_lanes, left, pltpu.roll(right, CAP, 1))
+        lower = jnp.where(low_lanes, pltpu.roll(left, CAP, 1), right)
         cols = slice(rows + p * LANES, rows + (p + 1) * LANES)
-        call_v[:, cols] = both[:SUB].astype(I32)
-        chosen = hot(iota((CAP, LANES), 0) + 1 == both[SUB : SUB + 1].astype(I32))
-        minus = lax.dot_general(
-            cent_ref[...], chosen, (((0,), (0,)), ((), ())), preferred_element_type=F32
-        )
-        xt_v[:, cols] = (-minus).astype(BF)
+        call_v[:codes_half, cols] = upper[:codes_half].astype(I32)
+        call_v[codes_half:, cols] = lower[:codes_half].astype(I32)
+        chosen = hot(iota((CAP, LANES), 0) + 1 == upper[codes_half : codes_half + 1].astype(I32))
+        picks.append(chosen)
         members = members + chosen.astype(F32)
+    xt_v[:, rows:] = dot(centt_v[...], jnp.concatenate(picks, 1)).astype(BF)
     tally_v[...] = jnp.broadcast_to(jnp.sum(members, axis=1, keepdims=True), (CAP, LANES))
 
     all_rows = call_v.shape[1]
@@ -244,7 +256,7 @@
         sums1(o).start()
         return carry
 
-    first, second = n_xc // 4 + 1, n_xc - 2
+    first, second = 2, n_xc - 2
     lax.fori_loop(1, first, remote_chunk, 0)
 
     own = tl_v[xc]
@@ -258,13 +270,6 @@
     ring_step(2)
     lax.fori_loop(first, second, remote_chunk, 0)
 
-    total = t2_b[y]
-    for o in range(1, n_y):
-        tally2(o).wait_recv()
-        total = total + t2_r[o]
-    t3_r[z] = total
-    for o in range(1, n_z):
-        tally3(o).start()
     ring_step(3)
     lax.fori_loop(second, n_xc, remote_chunk, 0)
     code_sums(0, own_v, F32)
@@ -279,8 +284,13 @@
         s2_b[d] = run
     for o in range(1, n_y):
         sums2(o).start()
-    for s in range(4, far + 1):
-        ring_step(s)
+    total = t2_b[y]
+    for o in range(1, n_y):
+        tally2(o).wait_recv()
+        total = total + t2_r[o]
+    t3_r[z] = total
+    for o in range(1, n_z):
+        tally3(o).start()
     run = s2_b[y]
     for o in range(1, n_y):
         sums2(o).wait_recv()
@@ -288,13 +298,8 @@
     s3_r[z] = run.astype(BF)
     for o in range(1, n_z):
         sums3(o).start()
-
-    lists = cent_ref[...].astype(F32) + ls_b[block(0)].astype(F32)
-    for up, slots in ((True, up_r), (False, down_r)):
-        ring(far, up).wait_recv()
-        lists = lists + slots[far - 1].astype(F32)
-    newc_ref[...] = lists * (1.0 / (1.0 + tally_v[:, :1]))
-
+    for s in range(4, far + 1):
+        ring_step(s)
     for o in range(1, n_z):
         tally3(o).wait_recv()
     for o in range(1, n_z):
@@ -306,6 +311,13 @@
     s4_r[xc] = run / (1.0 + total)
     for o in range(1, n_xc):
         sums4(o).start()
+
+    lists = cent_ref[...].astype(F32) + ls_b[block(0)].astype(F32)
+    for up, slots in ((True, up_r), (False, down_r)):
+        ring(far, up).wait_recv()
+        lists = lists + slots[far - 1].astype(F32)
+    newc_ref[...] = lists * (1.0 / (1.0 + tally_v[:, :1]))
+
     for o in range(1, n_xc):
         sums4(o).wait_recv()
     book_ref[...] = s4_r[...]
@@ -335,6 +347,8 @@
     share = SUB // n_y
     depth = din // K_PARTS
     sem = pltpu.SemaphoreType.DMA
+    slots = list_slot.reshape(1, rows)
+    operands = (route_counts, slots, pq_codes.T, centroids, pooled, proj_weight)
     vmem = pl.BlockSpec(memory_space=pltpu.VMEM)
     hbm = pl.BlockSpec(memory_space=pltpu.HBM)
     return pl.pallas_call(
@@ -362,8 +376,9 @@
             pltpu.VMEM((n_y, 1, CODES), F32),
             pltpu.VMEM((n_y, 1, CODES), F32),
             pltpu.VMEM((n_z, 1, CODES), F32),
-            pltpu.VMEM((n_y, SUB + 16, LANES), BF),
-            pltpu.VMEM((n_y, SUB + 16, LANES), BF),
+            pltpu.VMEM((n_y, SUB // 2 + 16, LANES), BF),
+            pltpu.VMEM((n_y, SUB // 2 + 16, LANES), BF),
+            pltpu.VMEM((features, CAP), BF),
             pltpu.VMEM((n_y * CAP, features), BF),
             pltpu.VMEM((far, CAP, features), BF),
             pltpu.VMEM((far, CAP, features), BF),
@@ -374,14 +389,15 @@
             pltpu.VMEM((n_y, SUBW, CODES), F32),
             pltpu.VMEM((n_z, SUBW, CODES), BF),
             pltpu.VMEM((n_xc, SUBW, CODES), F32),
-            sem((2, K_PARTS)), sem((4,)), sem((2, n_xc)), sem((2, n_y)), sem((2, n_z)),
-            sem((2, n_y)), sem((2, far)), sem((2, far)), sem((2, n_xc)), sem((2, n_y)), sem((2, n_z)), sem((2, n_xc)),
+            sem((2, K_PARTS)), sem((4,)), sem((2, n_xc)), sem((2, n_y)), sem((2, n_z)), sem((2, n_y)),
+            sem((2, far)), sem((2, far)), sem((2, n_xc)), sem((2, n_y)),
+            sem((2, n_z)), sem((2, n_xc)),
         ],
         compiler_params=pltpu.CompilerParams(
-            collective_id=0, has_side_effects=True, vmem_limit_bytes=63 << 20
+            collective_id=0, has_side_effects=True, vmem_limit_bytes=48 << 20
         ),
         name="step",
-    )(route_counts, list_slot.reshape(1, rows), pq_codes.T, centroids, pooled, proj_weight)
+    )(*(pltpu.with_memory_space_constraint(v, pltpu.HBM) for v in operands))
 
 
 def solution(mesh):

time: 64.2 us -> 57.9 us (0.902)
  Pallas kernels: 60.2 us -> 55.8 us
  local copies, waits for them, and re-layouts: 3.24 us -> 1.36 us
    pallas_call x1, Pallas kernels: 60.2 us -> 55.8 us  [local(): pl.pallas_call(functools.partial(kernel, n_z, n_xc, n_y), out_shape=(jax....]
    unnamed x2, local copies, waits for them, and re-layouts: 3.24 us -> 1.36 us
where the time goes in v4:
time: 57.9 us; the launch traced here: 57.8 us
  Pallas kernels  55.8 us (96%)
  local copies, waits for them, and re-layouts  1.36 us (2%)
  between operations  0.64 us (1%)
    pallas_call x1, Pallas kernels, local(): pl.pallas_call(functools.partial(kernel, n_z, n_xc, n_y), out_shape=(jax....  55.8 us
    unnamed x2, local copies, waits for them, and re-layouts  1.36 us

profile of v4, /device:TPU:1, one launch (start us, length us, event | category | flops | bytes accessed | tf_op | source)
XLA Modules:
  0.0 57.8 jit_solution(1480698649495323473)
XLA Ops:
  0.6 55.8 %step.1 = (f32[64,1024]{1,0:T(8,128)S(1)}, f32[8,16,256]{2,1,0:T(8,128)S(1)}) custom-call(s32[1,8]{1,0:T(1,128)} %counts_hbm.1, s32[1,256]{1,0:T(1,128)} %bitcast.3, s32[64,256]{1,0:T(8,128)} %bitcast.2, bf16[64,1024]{1,0:T(8,128)(2,1)} %cent_hbm.1, bf16[256,4096]{1,0:T(8,128)(2,1)} %pooled_hbm.1, bf16[4096,1024]{1,0:T(8,128)(2,1)} %weight_hbm.1), custom_call_target="tpu_custom_call" | custom-call | tf_op jit(solution)/shard_map/step/pallas_call | solution.py:354
  56.4 0.7 %copy.10 = f32[64,1024]{1,0:T(8,128)} copy(f32[64,1024]{1,0:T(8,128)S(1)} %get-tuple-element.4) | data formatting | bytes 524288
  57.1 0.7 %copy.11 = f32[8,16,256]{2,1,0:T(8,128)} copy(f32[8,16,256]{2,1,0:T(8,128)S(1)} %get-tuple-element.5) | data formatting | bytes 262144

commit v5 on v4

--- a/solution.py
+++ b/solution.py
@@ -33,6 +33,10 @@
 
 def dot_nt(a, b):
     return lax.dot_general(a, b, (((1,), (1,)), ((), ())), preferred_element_type=F32)
+
+
+def far_first(n):
+    return sorted(range(1, n), key=lambda o: -min(o, n - o))
 
 
 def kernel(
@@ -113,6 +117,14 @@
 
     def sums4(o):
         return send(s4_r.at[xc], s4_r.at[xc], s4_s, o, (at_xc(o), y))
+
+    barrier = pltpu.get_barrier_semaphore()
+    for o in far_first(n_y):
+        pl.semaphore_signal(barrier, inc=1, device_id=(dp, at_y(o)), device_id_type=MESH)
+    for o in far_first(n_xc):
+        pl.semaphore_signal(barrier, inc=1, device_id=(at_xc(o), y), device_id_type=MESH)
+    for o in range(1, n_z):
+        pl.semaphore_signal(barrier, inc=1, device_id=(at_z(o), y), device_id_type=MESH)
 
     small = [
         pltpu.make_async_copy(src, dst, small_sem.at[i])
@@ -138,14 +150,6 @@
         for copy in pair:
             copy.start()
         loads.append(pair)
-
-    barrier = pltpu.get_barrier_semaphore()
-    for o in range(1, n_xc):
-        pl.semaphore_signal(barrier, inc=1, device_id=(at_xc(o), y), device_id_type=MESH)
-    for o in range(1, n_y):
-        pl.semaphore_signal(barrier, inc=1, device_id=(dp, at_y(o)), device_id_type=MESH)
-    for o in range(1, n_z):
-        pl.semaphore_signal(barrier, inc=1, device_id=(at_z(o), y), device_id_type=MESH)
 
     for copy in small:
         copy.wait()
@@ -177,7 +181,7 @@
         cd_b[d] = packed[:, d * LANES : (d + 1) * LANES]
 
     pl.semaphore_wait(barrier, n_xc + n_y + n_z - 3)
-    for o in range(1, n_y):
+    for o in far_first(n_y):
         codes_out(o).start()
 
     centt_v[...] = (-cent_ref[...].astype(F32)).T.astype(BF)
@@ -251,13 +255,13 @@
             piece = xt_v[pl.ds(pl.multiple_of(m * SUBW, SUBW), SUBW)]
             out[d * SUBW : (d + 1) * SUBW] = dot_nt(piece, select).astype(kind)
 
-    def remote_chunk(o, carry):
-        code_sums(o, s1_b.at[o], BF)
-        sums1(o).start()
-        return carry
-
-    first, second = 2, n_xc - 2
-    lax.fori_loop(1, first, remote_chunk, 0)
+    def remote_chunks(offsets):
+        for o in offsets:
+            code_sums(o, s1_b.at[o], BF)
+            sums1(o).start()
+
+    order = far_first(n_xc)
+    remote_chunks(order[:1])
 
     own = tl_v[xc]
     for o in range(1, n_xc):
@@ -268,22 +272,23 @@
     for o in range(1, n_y):
         tally2(o).start()
     ring_step(2)
-    lax.fori_loop(first, second, remote_chunk, 0)
+    remote_chunks(order[1:5])
 
     ring_step(3)
-    lax.fori_loop(second, n_xc, remote_chunk, 0)
+    remote_chunks(order[5:])
     code_sums(0, own_v, F32)
 
     for o in range(1, n_xc):
         sums1(o).wait_recv()
-    for d in range(n_y):
-        part = slice(d * SUBW, (d + 1) * SUBW)
+    for o in far_first(n_y) + [0]:
+        d = at_y(o)
+        part = pl.ds(pl.multiple_of(d * SUBW, SUBW), SUBW)
         run = own_v[part]
-        for o in range(1, n_xc):
-            run = run + s1_r[o, part].astype(F32)
+        for i in range(1, n_xc):
+            run = run + s1_r[i, part].astype(F32)
         s2_b[d] = run
-    for o in range(1, n_y):
-        sums2(o).start()
+        if o:
+            sums2(o).start()
     total = t2_b[y]
     for o in range(1, n_y):
         tally2(o).wait_recv()
@@ -309,7 +314,7 @@
         total = total + t3_r[i]
         run = run + s3_r[i].astype(F32)
     s4_r[xc] = run / (1.0 + total)
-    for o in range(1, n_xc):
+    for o in far_first(n_xc):
         sums4(o).start()
 
     lists = cent_ref[...].astype(F32) + ls_b[block(0)].astype(F32)

time: 57.9 us -> 55.4 us (0.957)
  Pallas kernels: 55.8 us -> 53.2 us
    pallas_call x1, Pallas kernels: 55.8 us -> 53.2 us  [local(): pl.pallas_call(functools.partial(kernel, n_z, n_xc, n_y), out_shape=(jax....]
where the time goes in v5:
time: 55.4 us; the launch traced here: 55.2 us
  Pallas kernels  53.2 us (96%)
  local copies, waits for them, and re-layouts  1.36 us (2%)
  between operations  0.64 us (1%)
    pallas_call x1, Pallas kernels, local(): pl.pallas_call(functools.partial(kernel, n_z, n_xc, n_y), out_shape=(jax....  53.2 us
    unnamed x2, local copies, waits for them, and re-layouts  1.36 us

profile of v5, /device:TPU:1, one launch (start us, length us, event | category | flops | bytes accessed | tf_op | source)
XLA Modules:
  0.0 55.2 jit_solution(7221912794793704384)
XLA Ops:
  0.6 53.2 %step.1 = (f32[64,1024]{1,0:T(8,128)S(1)}, f32[8,16,256]{2,1,0:T(8,128)S(1)}) custom-call(s32[1,8]{1,0:T(1,128)} %counts_hbm.1, s32[1,256]{1,0:T(1,128)} %bitcast.3, s32[64,256]{1,0:T(8,128)} %bitcast.2, bf16[64,1024]{1,0:T(8,128)(2,1)} %cent_hbm.1, bf16[256,4096]{1,0:T(8,128)(2,1)} %pooled_hbm.1, bf16[4096,1024]{1,0:T(8,128)(2,1)} %weight_hbm.1), custom_call_target="tpu_custom_call" | custom-call | tf_op jit(solution)/shard_map/step/pallas_call | solution.py:359
  53.9 0.7 %copy.10 = f32[64,1024]{1,0:T(8,128)} copy(f32[64,1024]{1,0:T(8,128)S(1)} %get-tuple-element.4) | data formatting | bytes 524288
  54.6 0.7 %copy.11 = f32[8,16,256]{2,1,0:T(8,128)} copy(f32[8,16,256]{2,1,0:T(8,128)S(1)} %get-tuple-element.5) | data formatting | bytes 262144

commit v6 on v5

--- a/solution.py
+++ b/solution.py
@@ -261,7 +261,7 @@
             sums1(o).start()
 
     order = far_first(n_xc)
-    remote_chunks(order[:1])
+    remote_chunks(order[:3])
 
     own = tl_v[xc]
     for o in range(1, n_xc):
@@ -272,10 +272,8 @@
     for o in range(1, n_y):
         tally2(o).start()
     ring_step(2)
-    remote_chunks(order[1:5])
-
-    ring_step(3)
-    remote_chunks(order[5:])
+    remote_chunks(order[3:])
+
     code_sums(0, own_v, F32)
 
     for o in range(1, n_xc):
@@ -289,6 +287,7 @@
         s2_b[d] = run
         if o:
             sums2(o).start()
+    ring_step(3)
     total = t2_b[y]
     for o in range(1, n_y):
         tally2(o).wait_recv()

time: 55.4 us -> 53.2 us (0.960)
  Pallas kernels: 53.2 us -> 51.1 us
    pallas_call x1, Pallas kernels: 53.2 us -> 51.1 us  [local(): pl.pallas_call(functools.partial(kernel, n_z, n_xc, n_y), out_shape=(jax....]
where the time goes in v6:
time: 53.2 us; the launch traced here: 53.1 us
  Pallas kernels  51.1 us (96%)
  local copies, waits for them, and re-layouts  1.36 us (3%)
  between operations  0.64 us (1%)
    pallas_call x1, Pallas kernels, local(): pl.pallas_call(functools.partial(kernel, n_z, n_xc, n_y), out_shape=(jax....  51.1 us
    unnamed x2, local copies, waits for them, and re-layouts  1.36 us

profile of v6, /device:TPU:1, one launch (start us, length us, event | category | flops | bytes accessed | tf_op | source)
XLA Modules:
  0.0 53.1 jit_solution(12732757474391460776)
XLA Ops:
  0.6 51.1 %step.1 = (f32[64,1024]{1,0:T(8,128)S(1)}, f32[8,16,256]{2,1,0:T(8,128)S(1)}) custom-call(s32[1,8]{1,0:T(1,128)} %counts_hbm.1, s32[1,256]{1,0:T(1,128)} %bitcast.3, s32[64,256]{1,0:T(8,128)} %bitcast.2, bf16[64,1024]{1,0:T(8,128)(2,1)} %cent_hbm.1, bf16[256,4096]{1,0:T(8,128)(2,1)} %pooled_hbm.1, bf16[4096,1024]{1,0:T(8,128)(2,1)} %weight_hbm.1), custom_call_target="tpu_custom_call" | custom-call | tf_op jit(solution)/shard_map/step/pallas_call | solution.py:358
  51.7 0.7 %copy.10 = f32[64,1024]{1,0:T(8,128)} copy(f32[64,1024]{1,0:T(8,128)S(1)} %get-tuple-element.4) | data formatting | bytes 524288
  52.4 0.7 %copy.11 = f32[8,16,256]{2,1,0:T(8,128)} copy(f32[8,16,256]{2,1,0:T(8,128)S(1)} %get-tuple-element.5) | data formatting | bytes 262144

commit v7 on v6

--- a/solution.py
+++ b/solution.py
@@ -141,15 +141,12 @@
         copy.start()
     depth = weight_v.shape[1]
     loads = []
+    whole = pltpu.make_async_copy(pooled_hbm, pooled_v, in_sem.at[K_PARTS])
+    whole.start()
     for k in range(K_PARTS):
-        cols = pl.ds(k * depth, depth)
-        pair = (
-            pltpu.make_async_copy(pooled_hbm.at[:, cols], pooled_v.at[k], in_sem.at[0, k]),
-            pltpu.make_async_copy(weight_hbm.at[cols], weight_v.at[k], in_sem.at[1, k]),
-        )
-        for copy in pair:
-            copy.start()
-        loads.append(pair)
+        part = pl.ds(k * depth, depth)
+        loads.append(pltpu.make_async_copy(weight_hbm.at[part], weight_v.at[k], in_sem.at[k]))
+        loads[k].start()
 
     for copy in small:
         copy.wait()
@@ -205,9 +202,10 @@
         tally1(o).start()
 
     for k in range(K_PARTS):
-        for copy in loads[k]:
-            copy.wait()
-        part = dot(pooled_v[k], weight_v[k])
+        if k == 0:
+            whole.wait()
+        loads[k].wait()
+        part = dot(pooled_v[:, k * depth : (k + 1) * depth], weight_v[k])
         if k == 0:
             res_v[...] = part
         else:
@@ -368,7 +366,7 @@
             pltpu.VMEM((1, rows), I32),
             pltpu.VMEM((SUB, rows), I32),
             pltpu.VMEM(centroids.shape, BF),
-            pltpu.VMEM((K_PARTS, rows, depth), BF),
+            pltpu.VMEM((rows, din), BF),
             pltpu.VMEM((K_PARTS, depth, features), BF),
             pltpu.VMEM((rows, features), BF),
             pltpu.VMEM((features, all_rows), BF),
@@ -393,7 +391,7 @@
             pltpu.VMEM((n_y, SUBW, CODES), F32),
             pltpu.VMEM((n_z, SUBW, CODES), BF),
             pltpu.VMEM((n_xc, SUBW, CODES), F32),
-            sem((2, K_PARTS)), sem((4,)), sem((2, n_xc)), sem((2, n_y)), sem((2, n_z)), sem((2, n_y)),
+            sem((K_PARTS + 1,)), sem((4,)), sem((2, n_xc)), sem((2, n_y)), sem((2, n_z)), sem((2, n_y)),
             sem((2, far)), sem((2, far)), sem((2, n_xc)), sem((2, n_y)),
             sem((2, n_z)), sem((2, n_xc)),
         ],

time: 53.2 us -> 53.2 us (level)
  no operation moved by 1% of the time
where the time goes in v7:
time: 53.2 us; the launch traced here: 53 us
  Pallas kernels  51 us (96%)
  local copies, waits for them, and re-layouts  1.36 us (3%)
  between operations  0.64 us (1%)
    pallas_call x1, Pallas kernels, local(): pl.pallas_call(functools.partial(kernel, n_z, n_xc, n_y), out_shape=(jax....  51 us
    unnamed x2, local copies, waits for them, and re-layouts  1.36 us

profile of v7, /device:TPU:1, one launch (start us, length us, event | category | flops | bytes accessed | tf_op | source)
XLA Modules:
  0.0 53.0 jit_solution(4904450440525184774)
XLA Ops:
  0.6 51.0 %step.1 = (f32[64,1024]{1,0:T(8,128)S(1)}, f32[8,16,256]{2,1,0:T(8,128)S(1)}) custom-call(s32[1,8]{1,0:T(1,128)} %counts_hbm.1, s32[1,256]{1,0:T(1,128)} %bitcast.3, s32[64,256]{1,0:T(8,128)} %bitcast.2, bf16[64,1024]{1,0:T(8,128)(2,1)} %cent_hbm.1, bf16[256,4096]{1,0:T(8,128)(2,1)} %pooled_hbm.1, bf16[4096,1024]{1,0:T(8,128)(2,1)} %weight_hbm.1), custom_call_target="tpu_custom_call" | custom-call | tf_op jit(solution)/shard_map/step/pallas_call | solution.py:356
  51.7 0.7 %copy.10 = f32[64,1024]{1,0:T(8,128)} copy(f32[64,1024]{1,0:T(8,128)S(1)} %get-tuple-element.4) | data formatting | bytes 524288
  52.4 0.7 %copy.11 = f32[8,16,256]{2,1,0:T(8,128)} copy(f32[8,16,256]{2,1,0:T(8,128)S(1)} %get-tuple-element.5) | data formatting | bytes 262144
